TPU v7x, 128 devices: a whole 4x4x4 slice. The times are simulated.
128 devices in a mesh: ctx: 32 (over y, x, core), head: 4 (over z).
Axes of the slice: x: 4, y: 4, z: 4, core: 2. Of those that a mesh axis runs over, the one named last changes fastest.
Arguments:
- queries: bfloat16 [16384, 4096], P('ctx', 'head'), may hold values from -5 to 5
- keys: bfloat16 [16384, 512], P('ctx', 'head'), may hold values from -5 to 5
- values: bfloat16 [16384, 512], P('ctx', 'head'), may hold values from -6 to 6
- doc_ids: int32 [16384], replicated, may hold values from 0 to 31, never falling along the last dimension, each value on 1 to 1536 neighbouring positions
- out_weight: bfloat16 [4096, 8192], P(None, 'head'), may hold values from -0.09375 to 0.09375
Outputs:
- layer_out: bfloat16 [16384, 8192], P('ctx', 'head')
Inputs may be any that keep to these rules, and one draw needn't show every extreme that they name: `doc_ids`: every document holds at most 1536 tokens, and one holds exactly that many.
All inputs are finite; a program needn't handle non-finite values.
Results may differ from a plain program's by a relative error of at most 0.0053.
Values may be sent and summed in bfloat16 or wider, within the bound.
No kernel may reach another device: no remote copies, remote signals or barrier semaphores. Data moves between devices by JAX's collectives and lax.ppermute only.
A program may use at most 128 MiB of HBM per device.

v0:
```python
import jax
import jax.numpy as jnp
from jax import lax
from jax.sharding import PartitionSpec as P

HEAD_SIZE = 128
REACH = 3


def from_behind(block, axis, distance):
    devices = range(lax.axis_size(axis))
    route = [(i - distance, i) for i in devices if i - distance in devices]
    return lax.ppermute(block, axis, route)


def attend_window(queries, key_all, value_all, visible):
    rows_here = queries.shape[0]
    kv_heads = key_all.shape[1] // HEAD_SIZE
    group_width = queries.shape[1] // key_all.shape[1]
    local_span = key_all.shape[0]
    query_heads = queries.reshape(rows_here, kv_heads, group_width, HEAD_SIZE)
    key_heads = key_all.reshape(local_span, kv_heads, HEAD_SIZE)
    value_heads = value_all.reshape(local_span, kv_heads, HEAD_SIZE)
    scores = jnp.einsum(
        "qgjd,kgd->gjqk", query_heads, key_heads, preferred_element_type=jnp.float32
    ) * HEAD_SIZE ** (-0.5)
    masked = jnp.where(visible, scores, -jnp.inf)
    row_peak = jnp.max(masked, axis=3, keepdims=True)
    exponent = jnp.where(visible, jnp.exp(scores - row_peak), 0.0)
    row_total = jnp.sum(exponent, axis=3, keepdims=True)
    weights = exponent.astype(jnp.bfloat16)
    mixture = (
        jnp.einsum("gjqk,kgd->gjqd", weights, value_heads, preferred_element_type=jnp.float32)
        / row_total
    )
    return (
        jnp.transpose(mixture, (2, 0, 1, 3))
        .reshape(rows_here, queries.shape[1])
        .astype(jnp.bfloat16)
    )


def shards(queries, keys, values, doc_ids, out_weight):
    rows_here = keys.shape[0]
    shard_index = lax.axis_index("ctx")
    key_parts = []
    value_parts = []
    for offset in range(REACH, 0, -1):
        arrived = from_behind((keys, values), "ctx", offset)
        key_parts.append(arrived[0])
        value_parts.append(arrived[1])
    key_all = jnp.concatenate(key_parts + [keys], 0)
    value_all = jnp.concatenate(value_parts + [values], 0)
    local_span = key_all.shape[0]
    leading_rows = REACH * rows_here
    doc_pad = jnp.concatenate([jnp.full((leading_rows,), -1, jnp.int32), doc_ids], 0)
    first_row = shard_index * rows_here
    key_docs = lax.dynamic_slice_in_dim(doc_pad, first_row, local_span, 0)
    query_docs = lax.dynamic_slice_in_dim(doc_ids, first_row, rows_here, 0)
    key_rel = lax.iota(jnp.int32, local_span)
    query_rel = leading_rows + lax.iota(jnp.int32, rows_here)
    visible = (query_docs[:, None] == key_docs[None, :]) & (key_rel[None, :] <= query_rel[:, None])
    attended = attend_window(queries, key_all, value_all, visible)
    projected = jnp.dot(
        lax.all_gather(attended, "head", axis=1, tiled=True),
        out_weight,
        preferred_element_type=jnp.float32,
    )
    return projected.astype(jnp.bfloat16)


def solution(mesh):
    in_specs = (P("ctx", "head"), P("ctx", "head"), P("ctx", "head"), P(), P(None, "head"))
    out_specs = P("ctx", "head")
    return jax.shard_map(shards, mesh=mesh, in_specs=in_specs, out_specs=out_specs, check_vma=False)
```

profile of v0, /device:TPU:24, one launch (start us, length us, event | category | flops | bytes accessed | tf_op | source)
XLA Modules:
  0.0 143.9 jit_solution(6102187642814633350)
XLA Ops:
  6.5 0.0 copy-start
  6.5 0.0 all-gather.2.cloned.1.call-start
  6.5 1.1 copy.7
  7.6 1.9 %collective-permute-start.5 = (bf16[512,128]{0,1:T(8,128)(2,1)S(1)}, bf16[512,128]{0,1:T(8,128)(2,1)S(1)}, u32[]{:S(2)}, u32[]{:S(2)}) collective-permute-start(bf16[512,128]{0,1:T(8,128)(2,1)S(1)} %copy.7), channel_id=1, source_target_pairs={{0,4},{4,8},{8,12},{12,16},{16,20},{20,24},{24,28},{28,32},{32,36}... | collective-permute-start | bytes 393224 | tf_op jit(solution)/shard_map/ppermute | solution.py:13
  9.6 3.4 %collective-permute-start.4 = (bf16[512,128]{0,1:T(8,128)(2,1)S(1)}, bf16[512,128]{0,1:T(8,128)(2,1)S(1)}, u32[]{:S(2)}, u32[]{:S(2)}) collective-permute-start(bf16[512,128]{0,1:T(8,128)(2,1)S(1)} %copy.7), channel_id=1, source_target_pairs={{0,8},{4,12},{8,16},{12,20},{16,24},{20,28},{24,32},{28,36},{32,40... | collective-permute-start | bytes 393224 | tf_op jit(solution)/shard_map/ppermute | solution.py:13
  13.0 3.4 %collective-permute-start.1 = (bf16[512,128]{1,0:T(8,128)(2,1)}, bf16[512,128]{1,0:T(8,128)(2,1)S(1)}, u32[]{:S(2)}, u32[]{:S(2)}) collective-permute-start(bf16[512,128]{1,0:T(8,128)(2,1)} %param.6), channel_id=1, source_target_pairs={{0,8},{4,12},{8,16},{12,20},{16,24},{20,28},{24,32},{28,36},{32,40... | collective-permute-start | bytes 393224 | tf_op jit(solution)/shard_map/ppermute | solution.py:13
  16.4 2.5 %collective-permute-start = (bf16[512,128]{1,0:T(8,128)(2,1)}, bf16[512,128]{1,0:T(8,128)(2,1)S(1)}, u32[]{:S(2)}, u32[]{:S(2)}) collective-permute-start(bf16[512,128]{1,0:T(8,128)(2,1)} %param.6), channel_id=1, source_target_pairs={{0,12},{4,16},{8,20},{12,24},{16,28},{20,32},{24,36},{28,40},{32,4... | collective-permute-start | bytes 393224 | tf_op jit(solution)/shard_map/ppermute | solution.py:13
  18.9 2.6 %collective-permute-start.2 = (bf16[512,128]{1,0:T(8,128)(2,1)}, bf16[512,128]{1,0:T(8,128)(2,1)S(1)}, u32[]{:S(2)}, u32[]{:S(2)}) collective-permute-start(bf16[512,128]{1,0:T(8,128)(2,1)} %param.6), channel_id=1, source_target_pairs={{0,4},{4,8},{8,12},{12,16},{16,20},{20,24},{24,28},{28,32},{32,36}... | collective-permute-start | bytes 393224 | tf_op jit(solution)/shard_map/ppermute | solution.py:13
  21.6 0.8 dynamic_slice.6
  22.4 0.8 pad_dynamic-slice_fusion
  23.2 0.9 fusion.9
  24.1 0.0 collective-permute-done.1
  24.1 1.9 %collective-permute-start.3 = (bf16[512,128]{0,1:T(8,128)(2,1)S(1)}, bf16[512,128]{0,1:T(8,128)(2,1)S(1)}, u32[]{:S(2)}, u32[]{:S(2)}) collective-permute-start(bf16[512,128]{0,1:T(8,128)(2,1)S(1)} %copy.7), channel_id=1, source_target_pairs={{0,12},{4,16},{8,20},{12,24},{16,28},{20,32},{24,36},{28,40},{32,4... | collective-permute-start | bytes 393224 | tf_op jit(solution)/shard_map/ppermute | solution.py:13
  26.1 0.0 collective-permute-done
  26.1 2.0 %collective-permute-done.2 = bf16[512,128]{1,0:T(8,128)(2,1)S(1)} collective-permute-done((bf16[512,128]{1,0:T(8,128)(2,1)}, bf16[512,128]{1,0:T(8,128)(2,1)S(1)}, u32[]{:S(2)}, u32[]{:S(2)}) %collective-permute-start.2) | collective-permute-done | bytes 131104 | tf_op jit(solution)/shard_map/ppermute | solution.py:13
  28.1 14.3 %fusion = (f32[8,512]{1,0:T(8,128)S(1)}, f32[2048,512,8]{1,0,2:T(8,128)}) fusion(pred[512,2048]{0,1:T(8,128)(4,1)S(1)} %fusion.9, bf16[512,128]{1,0:T(8,128)(2,1)} %param.6, bf16[512,128]{1,0:T(8,128)(2,1)S(1)} %collective-permute-done.2, bf16[512,128]{1,0:T(8,128)(2,1)S(1)} %collective-permute-done.1, bf16[512,128]{1,0:T(8,128)(2,1)S(1)} %collective-permute-done, ...), kind=kOutput, calls=%fused_computation.2 | convolution fusion | flops 2174742528 | bytes 36192256 | tf_op jit(solution)/shard_map/qgjd,kgd->gjqk/dot_general | solution.py:24
  42.4 14.4 %fusion.3 = f32[8,512]{1,0:T(8,128)S(1)} fusion(f32[2048,512,8]{1,0,2:T(8,128)} %get-tuple-element.6, f32[8,512]{1,0:T(8,128)S(1)} %get-tuple-element.5, pred[512,2048]{0,1:T(8,128)(4,1)S(1)} %fusion.9), kind=kLoop, calls=%fused_computation.5 | loop fusion | flops 33550336 | bytes 34635776 | tf_op jit(solution)/shard_map/reduce_sum | solution.py:30
  56.8 0.0 collective-permute-done.5
  56.8 0.0 collective-permute-done.4
  56.8 0.0 collective-permute-done.3
  56.8 15.5 %divide_convert_fusion = bf16[8,512,128]{1,2,0:T(8,128)(2,1)} fusion(f32[8,512]{1,0:T(8,128)S(1)} %fusion.3, f32[2048,512,8]{1,0,2:T(8,128)} %get-tuple-element.6, f32[8,512]{1,0:T(8,128)S(1)} %get-tuple-element.5, pred[512,2048]{0,1:T(8,128)(4,1)S(1)} %fusion.9, bf16[512,128]{0,1:T(8,128)(2,1)S(1)} %copy.7, ...), kind=kOutput, calls=%fused_computation.13 | convolution fusion | flops 2184183808 | bytes 36208640 | tf_op jit(solution)/shard_map/gjqk,kgd->gjqd/dot_general | solution.py:33
  72.3 0.0 all-gather.2.cloned.1.call-update
  72.4 50.1 %all-gather.2.cloned.1.call-done = bf16[512,4096]{0,1:T(8,128)(2,1)} async-done(((bf16[512,1024]{0,1:T(8,128)(2,1)}), bf16[512,4096]{0,1:T(8,128)(2,1)}) %all-gather.2.cloned.1.call-update) | async-done | bytes 4194320 | tf_op jit(solution)/shard_map/all_gather | solution.py:65
  122.5 14.6 %convolution_convert_fusion = bf16[512,2048]{1,0:T(8,128)(2,1)} fusion(bf16[512,4096]{0,1:T(8,128)(2,1)} %all-gather.2.cloned.1.call-done, bf16[4096,2048]{1,0:T(8,128)(2,1)} %param.9), kind=kOutput, calls=%fused_computation.12 | convolution fusion | flops 8590983168 | bytes 23068672 | tf_op jit(solution)/shard_map/dot_general | solution.py:64
  (2 shorter events, 0.0 us)
Async XLA Ops:
  6.5 21.6 %copy-start = (bf16[512,1024]{1,0:T(8,128)(2,1)S(1)}, bf16[512,1024]{1,0:T(8,128)(2,1)}, u32[]{:S(2)}) copy-start(bf16[512,1024]{1,0:T(8,128)(2,1)} %param.5) | copy-start | bytes 3145732
  6.5 116.0 %all-gather.2.cloned.1.call-start = ((), (), s32[]{:S(2)}) async-start(), calls=%async_computation | async-start | bytes 5242880 | tf_op jit(solution)/shard_map/all_gather | solution.py:65
  7.6 49.2 %collective-permute-start.5 = (bf16[512,128]{0,1:T(8,128)(2,1)S(1)}, bf16[512,128]{0,1:T(8,128)(2,1)S(1)}, u32[]{:S(2)}, u32[]{:S(2)}) collective-permute-start(bf16[512,128]{0,1:T(8,128)(2,1)S(1)} %copy.7), channel_id=1, source_target_pairs={{0,4},{4,8},{8,12},{12,16},{16,20},{20,24},{24,28},{28,32},{32,36}... | collective-permute-start | bytes 393224 | tf_op jit(solution)/shard_map/ppermute | solution.py:13
  9.6 47.3 %collective-permute-start.4 = (bf16[512,128]{0,1:T(8,128)(2,1)S(1)}, bf16[512,128]{0,1:T(8,128)(2,1)S(1)}, u32[]{:S(2)}, u32[]{:S(2)}) collective-permute-start(bf16[512,128]{0,1:T(8,128)(2,1)S(1)} %copy.7), channel_id=1, source_target_pairs={{0,8},{4,12},{8,16},{12,20},{16,24},{20,28},{24,32},{28,36},{32,40... | collective-permute-start | bytes 393224 | tf_op jit(solution)/shard_map/ppermute | solution.py:13
  13.0 11.1 %collective-permute-start.1 = (bf16[512,128]{1,0:T(8,128)(2,1)}, bf16[512,128]{1,0:T(8,128)(2,1)S(1)}, u32[]{:S(2)}, u32[]{:S(2)}) collective-permute-start(bf16[512,128]{1,0:T(8,128)(2,1)} %param.6), channel_id=1, source_target_pairs={{0,8},{4,12},{8,16},{12,20},{16,24},{20,28},{24,32},{28,36},{32,40... | collective-permute-start | bytes 393224 | tf_op jit(solution)/shard_map/ppermute | solution.py:13
  16.4 9.7 %collective-permute-start = (bf16[512,128]{1,0:T(8,128)(2,1)}, bf16[512,128]{1,0:T(8,128)(2,1)S(1)}, u32[]{:S(2)}, u32[]{:S(2)}) collective-permute-start(bf16[512,128]{1,0:T(8,128)(2,1)} %param.6), channel_id=1, source_target_pairs={{0,12},{4,16},{8,20},{12,24},{16,28},{20,32},{24,36},{28,40},{32,4... | collective-permute-start | bytes 393224 | tf_op jit(solution)/shard_map/ppermute | solution.py:13
  18.9 9.2 %collective-permute-start.2 = (bf16[512,128]{1,0:T(8,128)(2,1)}, bf16[512,128]{1,0:T(8,128)(2,1)S(1)}, u32[]{:S(2)}, u32[]{:S(2)}) collective-permute-start(bf16[512,128]{1,0:T(8,128)(2,1)} %param.6), channel_id=1, source_target_pairs={{0,4},{4,8},{8,12},{12,16},{16,20},{20,24},{24,28},{28,32},{32,36}... | collective-permute-start | bytes 393224 | tf_op jit(solution)/shard_map/ppermute | solution.py:13
  24.1 32.7 %collective-permute-start.3 = (bf16[512,128]{0,1:T(8,128)(2,1)S(1)}, bf16[512,128]{0,1:T(8,128)(2,1)S(1)}, u32[]{:S(2)}, u32[]{:S(2)}) collective-permute-start(bf16[512,128]{0,1:T(8,128)(2,1)S(1)} %copy.7), channel_id=1, source_target_pairs={{0,12},{4,16},{8,20},{12,24},{16,28},{20,32},{24,36},{28,40},{32,4... | collective-permute-start | bytes 393224 | tf_op jit(solution)/shard_map/ppermute | solution.py:13
Sparse Core Ops, SparseCore 0:
  72.5 49.9 all-gather.1
where the time goes:
time: 145 us; the launch traced here: 144 us
  waiting for transfers between devices  52.2 us (36%)
  matrix products  44.4 us (31%)
  starting transfers between devices  15.8 us (11%)
  other arithmetic  15.3 us (11%)
  between operations  13.5 us (9%)
  local copies, waits for them, and re-layouts  2.65 us (2%)
    all_gather x1, waiting for transfers between devices, shards(): lax.all_gather(attended, 'head', axis=1, tiled=True)  50.1 us
    ppermute x6, starting transfers between devices, from_behind(): return lax.ppermute(block, axis, route)  15.8 us
    dot_general x1, matrix products, attend_window(): jnp.einsum('gjqk,kgd->gjqd', weights, value_heads, preferred_element_type...  15.5 us
    dot_general x1, matrix products, shards(): jnp.dot(lax.all_gather(attended, 'head', axis=1, tiled=True), out_weight,...  14.6 us
    reduce_sum x1, other arithmetic, attend_window(): row_total = jnp.sum(exponent, axis=3, keepdims=True)  14.4 us
    dot_general x1, matrix products, attend_window(): jnp.einsum('qgjd,kgd->gjqk', query_heads, key_heads, preferred_element_ty...  14.3 us
  transfers between devices with their start and end apart: 7, of which 2 were waited for; matrix products, arithmetic and copies ran while one was open for 22% of the time, Pallas kernels for 0%

commit v1 on v0

v1 whole, which is shorter than its diff:
```python
import functools
import math

import jax
import jax.numpy as jnp
from jax import lax
from jax.experimental import pallas as pl
from jax.experimental.pallas import tpu as pltpu
from jax.sharding import PartitionSpec as P

HEAD_SIZE = 128
REACH = 3
EXPONENT_SCALE = math.log2(math.e) * HEAD_SIZE ** (-0.5)
HIDDEN = -1e30
CONTRACT_LAST = (((1,), (1,)), ((), ()))
PLAIN = (((1,), (0,)), ((), ()))
VMEM = pl.BlockSpec(memory_space=pltpu.VMEM)
SMEM = pl.BlockSpec(memory_space=pltpu.SMEM)


def beside_ones(values):
    return jnp.concatenate([values, jnp.ones_like(values)], 1)


def wide(column, count):
    return column if count == 1 else jnp.concatenate([column] * count, 1)


def block_update(q, keys, values, bias, before, mixed):
    span = keys.shape[0]
    s = lax.dot_general(q, keys, CONTRACT_LAST, preferred_element_type=jnp.float32)
    if bias is not None:
        s = s + bias
    peak = jnp.broadcast_to(jnp.max(s, axis=1, keepdims=True), (q.shape[0], HEAD_SIZE))
    if before is not None:
        peak = jnp.maximum(before, peak)
    weights = jnp.exp2((s - wide(peak, span // HEAD_SIZE)) * EXPONENT_SCALE).astype(jnp.bfloat16)
    mix = lax.dot_general(weights, beside_ones(values), PLAIN, preferred_element_type=jnp.float32)
    if before is not None:
        mix = mix + mixed * wide(jnp.exp2((before - peak) * EXPONENT_SCALE), 2)
    return peak, mix


def own_kernel(q_ref, own_ref, qdoc_ref, kdoc_ref, peak_ref, mix_ref, bias_ref):
    rows = q_ref.shape[0]
    half = rows // 2
    heads = q_ref.shape[1] // HEAD_SIZE
    own_at = REACH * rows
    for part in range(2):
        span = (part + 1) * half
        at = part * half
        row = at + lax.broadcasted_iota(jnp.int32, (half, span), 0)
        col = lax.broadcasted_iota(jnp.int32, (half, span), 1)
        doc = wide(qdoc_ref[at:at + half, :], span // HEAD_SIZE)
        seen = (doc == kdoc_ref[0:1, own_at:own_at + span]) & (col <= row)
        bias_ref[:, 0:span] = jnp.where(seen, 0.0, HIDDEN)
        for head in range(heads):
            q = q_ref[at:at + half, head * HEAD_SIZE:(head + 1) * HEAD_SIZE]
            peak, mix = block_update(q, own_ref[0:span, :], own_ref[rows:rows + span, :], bias_ref[:, 0:span], None, None)
            peak_ref[head, at:at + half, :] = peak
            mix_ref[head, at:at + half, :] = mix


def rest_kernel(first_head, heads, edge_ref, q_ref, peak_ref, mix_ref, k1_ref, k2_ref, k3_ref, qdoc_ref, kdoc_ref,
                out_ref, peak_now, mix_now, bias_ref):
    rows = q_ref.shape[0]
    half = rows // 2
    peak_now[...] = peak_ref[first_head:first_head + heads]
    mix_now[...] = mix_ref[first_head:first_head + heads]

    def update(part, ref, at, span, window_at, masked):
        here = slice(part * half, (part + 1) * half)
        if masked:
            doc = wide(qdoc_ref[here, :], span // HEAD_SIZE)
            bias_ref[:, 0:span] = jnp.where(doc == kdoc_ref[0:1, window_at:window_at + span], 0.0, HIDDEN)
        for head in range(heads):
            column = (first_head + head) * HEAD_SIZE
            peak, mix = block_update(
                q_ref[here, column:column + HEAD_SIZE], ref[at:at + span, :], ref[rows + at:rows + at + span, :],
                bias_ref[:, 0:span] if masked else None, peak_now[head, here, :], mix_now[head, here, :])
            peak_now[head, here, :] = peak
            mix_now[head, here, :] = mix

    for part in range(2):
        first_doc = edge_ref[2 * (2 * REACH + part)]
        last_doc = edge_ref[2 * (2 * REACH + part) + 1]
        for ref, shard, pieces in ((k1_ref, 2, ((0, rows),)), (k2_ref, 1, ((0, rows),)), (k3_ref, 0, ((half, half), (0, half)))):
            for at, span in pieces:
                lo = edge_ref[2 * (2 * shard + at // half)]
                hi = edge_ref[2 * (2 * shard + (at + span) // half - 1) + 1]
                window_at = shard * rows + at

                @pl.when((hi == first_doc) & (lo == last_doc))
                def _():
                    update(part, ref, at, span, window_at, False)

                @pl.when((hi == first_doc) & (lo != last_doc))
                def _():
                    update(part, ref, at, span, window_at, True)

    for head in range(heads):
        mix = mix_now[head, :, 0:HEAD_SIZE] / mix_now[head, :, HEAD_SIZE:]
        out_ref[:, head * HEAD_SIZE:(head + 1) * HEAD_SIZE] = mix.astype(jnp.bfloat16)


def attend_own(queries, own, qdoc, kdoc):
    rows, width = queries.shape
    heads = width // HEAD_SIZE
    return pl.pallas_call(
        own_kernel,
        in_specs=[VMEM] * 4,
        out_specs=[VMEM] * 2,
        scratch_shapes=[pltpu.VMEM((rows // 2, rows), jnp.float32)],
        out_shape=[
            jax.ShapeDtypeStruct((heads, rows, HEAD_SIZE), jnp.float32),
            jax.ShapeDtypeStruct((heads, rows, 2 * HEAD_SIZE), jnp.float32),
        ],
        compiler_params=pltpu.CompilerParams(vmem_limit_bytes=8 * 2**20),
        cost_estimate=pl.CostEstimate(flops=2**32, bytes_accessed=2**20, transcendentals=2**20),
        name="attend_own",
    )(queries, own, qdoc, kdoc)


def attend_rest(queries, state, parts, qdoc, kdoc, edges, first_head, heads):
    rows = queries.shape[0]
    return pl.pallas_call(
        functools.partial(rest_kernel, first_head, heads),
        in_specs=[SMEM] + [VMEM] * 8,
        out_specs=VMEM,
        scratch_shapes=[
            pltpu.VMEM((heads, rows, HEAD_SIZE), jnp.float32),
            pltpu.VMEM((heads, rows, 2 * HEAD_SIZE), jnp.float32),
            pltpu.VMEM((rows // 2, rows), jnp.float32),
        ],
        out_shape=jax.ShapeDtypeStruct((rows, heads * HEAD_SIZE), jnp.bfloat16),
        compiler_params=pltpu.CompilerParams(vmem_limit_bytes=10 * 2**20),
        cost_estimate=pl.CostEstimate(flops=2**32, bytes_accessed=2**20, transcendentals=2**20),
        name=f"attend_rest_{first_head}",
    )(edges, queries, *state, *parts, qdoc, kdoc)


def project_kernel(counts, carried, at_ref, *refs):
    weight_refs, out_ref = refs[-1 - len(counts):-1], refs[-1]
    total = refs[sum(counts)][...] if carried else None
    n = 0
    for count, weight_ref in zip(counts, weight_refs):
        pieces = [refs[n + j][...] for j in range(count)]
        n += count
        left = pieces[0] if count == 1 else jnp.concatenate(pieces, 1)
        term = lax.dot_general(left, weight_ref[...], PLAIN, preferred_element_type=jnp.float32)
        total = term if total is None else total + term
    out_ref[...] = total.astype(out_ref.dtype)


def project(terms, at, weight, carried, out_dtype, name, columns=512, vmem=48):
    rows = terms[0][0].shape[0]
    width = weight.shape[1]
    depth = sum(piece.shape[1] for piece in terms[0])
    pieces = [piece for term in terms for piece in term]
    tile = pl.BlockSpec((rows, columns), lambda n, at: (0, n))
    weights = [pl.BlockSpec((depth, columns), lambda n, at, i=i: (at[i], n)) for i in range(len(terms))]
    return pl.pallas_call(
        functools.partial(project_kernel, tuple(len(t) for t in terms), carried is not None),
        grid_spec=pltpu.PrefetchScalarGridSpec(
            num_scalar_prefetch=1,
            grid=(width // columns,),
            in_specs=[VMEM] * len(pieces) + ([tile] if carried is not None else []) + weights,
            out_specs=tile,
        ),
        out_shape=jax.ShapeDtypeStruct((rows, width), out_dtype),
        compiler_params=pltpu.CompilerParams(vmem_limit_bytes=vmem * 2**20),
        cost_estimate=pl.CostEstimate(flops=2**20, bytes_accessed=2**10, transcendentals=0),
        name=name,
    )(jnp.stack(at).astype(jnp.int32), *pieces, *([carried] if carried is not None else []), *[weight] * len(terms))


def once_here(value, *others):
    anywhere = pl.BlockSpec(memory_space=pl.ANY)
    return pl.pallas_call(
        lambda *refs: None,
        in_specs=[anywhere] * (1 + len(others)),
        out_specs=anywhere,
        out_shape=jax.ShapeDtypeStruct(value.shape, value.dtype),
        input_output_aliases={0: 0},
        compiler_params=pltpu.CompilerParams(vmem_limit_bytes=2**20),
        cost_estimate=pl.CostEstimate(flops=0, bytes_accessed=0, transcendentals=0),
        name="once_here",
    )(value, *others)


def shards(queries, keys, values, doc_ids, out_weight):
    rows = keys.shape[0]
    shard = lax.axis_index("ctx")
    place = lax.axis_index("head")
    shard_count = lax.axis_size("ctx")
    places = lax.axis_size("head")
    other_core = [(i, i ^ 1) for i in range(shard_count)]

    def along_ctx(block, pairs):
        return lax.ppermute(block, "ctx", pairs)

    def along_head(block, step):
        return lax.ppermute(block, "head", [(i, (i + step) % places) for i in range(places)])

    own = jnp.concatenate([keys, values], 0)
    two_behind = along_ctx(own, [(i, i + 2) for i in range(shard_count - 2)])
    three_behind = along_ctx(own, [(i, i + 3) for i in range(1, shard_count - 3, 2)])
    beside = along_ctx(own, other_core)
    window = (REACH + 1) * rows
    padded = jnp.concatenate([jnp.full((REACH * rows,), -1, jnp.int32), doc_ids], 0)
    kdoc = lax.dynamic_slice_in_dim(padded, shard * rows, window, 0)
    half = rows // 2
    edges = jnp.stack([kdoc[::half], kdoc[half - 1::half]], 1).reshape(-1)
    qdoc = jnp.broadcast_to(kdoc[REACH * rows:, None], (rows, HEAD_SIZE))
    kdoc = kdoc[None, :]

    state = attend_own(queries, own, qdoc, kdoc)
    beside_two = along_ctx(two_behind, other_core)
    is_second = (shard % 2) == 1
    part1 = jnp.where(is_second, beside, beside_two)
    part2 = two_behind
    part3 = jnp.where(is_second, beside_two, three_behind)

    parts = (part1, part2, part3)
    split = 5
    a = attend_rest(queries, state, parts, qdoc, kdoc, edges, 0, split)
    a_up = along_head(a, 1)
    a_down = along_head(a, -1)
    b = attend_rest(queries, state, parts, qdoc, kdoc, edges, split, 8 - split)
    b_up = along_head(b, 1)
    b_down = along_head(b, -1)
    below = (place + places - 1) % places
    above = (place + 1) % places
    far = (place + 2) % places
    a_far = along_head(a_up, 1)
    b_down = once_here(b_down, a_down, b_up)
    b_far = along_head(b_down, -1)
    total = project([(a, b), (a_up, b_up), (a_down, b_down)], [place, below, above], out_weight, None, jnp.float32, "project_near")
    return project([(a_far, b_far)], [far], out_weight, total, jnp.bfloat16, "project_far", vmem=56)


def solution(mesh):
    in_specs = (P("ctx", "head"), P("ctx", "head"), P("ctx", "head"), P(), P(None, "head"))
    out_specs = P("ctx", "head")
    return jax.shard_map(shards, mesh=mesh, in_specs=in_specs, out_specs=out_specs, check_vma=False)
```

time: 145 us -> 76.8 us (0.53); the launches traced: 144 us -> 77.6 us
  matrix products: 44.4 us -> 0 us
  Pallas kernels: 0 us -> 33.3 us
  waiting for transfers between devices: 52.2 us -> 19.8 us
  other arithmetic: 15.3 us -> 0.14 us
  between operations: 13.5 us -> 0.12 us
  local copies, waits for them, and re-layouts: 2.65 us -> 5.85 us
  starting transfers between devices: 15.8 us -> 18.4 us
    all_gather x1 -> x0, waiting for transfers between devices: 50.1 us -> none  [shards(): lax.all_gather(attended, 'head', axis=1, tiled=True)]
    dot_general x3 -> x0, matrix products: 44.4 us -> none  [the longest x1 15.5 us: attend_window(): jnp.einsum('gjqk,kgd->gjqd', weights, value_heads, preferred_element_type...]
    pallas_call x0 -> x6, Pallas kernels: none -> 33.3 us  [the longest x2 17.9 us: project(): pl.pallas_call(functools.partial(project_kernel, tuple((len(t) for t in t...]
    ppermute x6 -> x10, waiting for transfers between devices: 2.05 us -> 19.8 us  [the longest x6 15.1 us: along_head(): lax.ppermute(block, 'head', [(i, (i + step) % places) for i in range(plac...]
    reduce_sum x1 -> x0, other arithmetic: 14.4 us -> none  [attend_window(): row_total = jnp.sum(exponent, axis=3, keepdims=True)]
    ppermute x6 -> x10, starting transfers between devices: 15.8 us -> 18.4 us  [the longest x6 9.57 us: along_head(): lax.ppermute(block, 'head', [(i, (i + step) % places) for i in range(plac...]
    unnamed x3 -> x7, local copies, waits for them, and re-layouts: 1.1 us -> 2.89 us
  transfers between devices with their start and end apart: 7 -> 10, of which waited for: 2 -> 3; matrix products, arithmetic and copies ran while one was open for 22% -> 3% of each run, Pallas kernels for 0% -> 25%
where the time goes in v1:
time: 76.8 us; the launch traced here: 77.6 us
  Pallas kernels  33.3 us (43%)
  waiting for transfers between devices  19.8 us (26%)
  starting transfers between devices  18.4 us (24%)
  local copies, waits for them, and re-layouts  5.85 us (8%)
    pallas_call x2, Pallas kernels, project(): pl.pallas_call(functools.partial(project_kernel, tuple((len(t) for t in t...  17.9 us
    ppermute x6, waiting for transfers between devices, along_head(): lax.ppermute(block, 'head', [(i, (i + step) % places) for i in range(plac...  15.1 us
    pallas_call x2, Pallas kernels, attend_rest(): pl.pallas_call(functools.partial(rest_kernel, first_head, heads), in_spec...  13.1 us
    ppermute x6, starting transfers between devices, along_head(): lax.ppermute(block, 'head', [(i, (i + step) % places) for i in range(plac...  9.57 us
    ppermute x4, starting transfers between devices, along_ctx(): return lax.ppermute(block, 'ctx', pairs)  8.82 us
    ppermute x4, waiting for transfers between devices, along_ctx(): return lax.ppermute(block, 'ctx', pairs)  4.77 us
    unnamed x7, local copies, waits for them, and re-layouts  2.89 us
    pallas_call x1, Pallas kernels, attend_own(): pl.pallas_call(own_kernel, in_specs=[VMEM] * 4, out_specs=[VMEM] * 2, scr...  2.31 us
  transfers between devices with their start and end apart: 10, of which 3 were waited for; matrix products, arithmetic and copies ran while one was open for 3% of the time, Pallas kernels for 25%

profile of v1, /device:TPU:24, one launch (start us, length us, event | category | flops | bytes accessed | tf_op | source)
XLA Modules:
  0.0 77.6 jit_solution(10851059112556589576)
XLA Ops:
  0.0 0.9 %constant_dynamic-update-slice_fusion.1 = bf16[1024,128]{1,0:T(8,128)(2,1)S(1)} fusion(bf16[512,128]{1,0:T(8,128)(2,1)} %param.6), kind=kLoop, calls=%fused_computation.5 | loop fusion | bytes 262144
  0.9 0.9 %constant_dynamic-update-slice_fusion.own_ref = bf16[1024,128]{1,0:T(8,128)(2,1)S(1)} fusion(bf16[1024,128]{1,0:T(8,128)(2,1)S(1)} %constant_dynamic-update-slice_fusion.1, bf16[512,128]{1,0:T(8,128)(2,1)} %param.7), kind=kLoop, calls=%fused_computation.4 | loop fusion | bytes 262144 | tf_op jit(solution)/shard_map/concatenate | solution.py:205
  1.8 1.3 %collective-permute-start.3 = (bf16[1024,128]{1,0:T(8,128)(2,1)S(1)}, bf16[1024,128]{1,0:T(8,128)(2,1)S(1)}, u32[]{:S(2)}, u32[]{:S(2)}) collective-permute-start(bf16[1024,128]{1,0:T(8,128)(2,1)S(1)} %constant_dynamic-update-slice_fusion.own_ref), channel_id=1, source_target_pairs={{4,16},{12,24},{20,32},{28,40},{36,48},{44,56},{52,64},{60,72},{68... | collective-permute-start | bytes 786440 | tf_op jit(solution)/shard_map/ppermute | solution.py:200
  3.1 3.4 %collective-permute-start.1 = (bf16[1024,128]{1,0:T(8,128)(2,1)S(1)}, bf16[1024,128]{1,0:T(8,128)(2,1)S(1)}, u32[]{:S(2)}, u32[]{:S(2)}) collective-permute-start(bf16[1024,128]{1,0:T(8,128)(2,1)S(1)} %constant_dynamic-update-slice_fusion.own_ref), channel_id=1, source_target_pairs={{0,8},{4,12},{8,16},{12,20},{16,24},{20,28},{24,32},{28,36},{32,40... | collective-permute-start | bytes 786440 | tf_op jit(solution)/shard_map/ppermute | solution.py:200
  6.6 2.7 %collective-permute-start = (bf16[1024,128]{1,0:T(8,128)(2,1)S(1)}, bf16[1024,128]{1,0:T(8,128)(2,1)S(1)}, u32[]{:S(2)}, u32[]{:S(2)}) collective-permute-start(bf16[1024,128]{1,0:T(8,128)(2,1)S(1)} %constant_dynamic-update-slice_fusion.own_ref), channel_id=1, source_target_pairs={{0,4},{4,0},{8,12},{12,8},{16,20},{20,16},{24,28},{28,24},{32,36},... | collective-permute-start | bytes 786440 | tf_op jit(solution)/shard_map/ppermute | solution.py:200
  9.2 0.8 %pad_dynamic-slice_fusion.1 = s32[2048]{0:T(1024)S(1)} fusion(s32[]{:T(128)S(6)} %select_n.35, s32[16384]{0:T(1024)} %param.8), kind=kLoop, calls=%fused_computation.3 | loop fusion | bytes 73732 | tf_op jit(solution)/shard_map/dynamic_slice | solution.py:211
  10.0 0.1 slice.10
  10.4 0.8 %pad_dynamic-slice_fusion = s32[512]{0:T(512)S(1)} fusion(s32[]{:T(128)S(6)} %add.38, s32[16384]{0:T(1024)} %param.8), kind=kLoop, calls=%fused_computation.2 | loop fusion | bytes 67588 | tf_op jit(solution)/shard_map/slice | solution.py:214
  11.2 4.8 %collective-permute-done.1.k2_ref = bf16[1024,128]{1,0:T(8,128)(2,1)S(1)} collective-permute-done((bf16[1024,128]{1,0:T(8,128)(2,1)S(1)}, bf16[1024,128]{1,0:T(8,128)(2,1)S(1)}, u32[]{:S(2)}, u32[]{:S(2)}) %collective-permute-start.1) | collective-permute-done | bytes 262176 | tf_op jit(solution)/shard_map/ppermute | solution.py:200
  15.9 1.5 %collective-permute-start.2 = (bf16[1024,128]{1,0:T(8,128)(2,1)S(1)}, bf16[1024,128]{1,0:T(8,128)(2,1)S(1)}, u32[]{:S(2)}, u32[]{:S(2)}) collective-permute-start(bf16[1024,128]{1,0:T(8,128)(2,1)S(1)} %collective-permute-done.1.k2_ref), channel_id=1, source_target_pairs={{0,4},{4,0},{8,12},{12,8},{16,20},{20,16},{24,28},{28,24},{32,36},... | collective-permute-start | bytes 786440 | tf_op jit(solution)/shard_map/ppermute | solution.py:200
  17.4 0.1 broadcast_in_dim.4.qdoc_ref
  17.5 1.2 %copy-done = bf16[512,1024]{1,0:T(8,128)(2,1)S(1)} copy-done((bf16[512,1024]{1,0:T(8,128)(2,1)S(1)}, bf16[512,1024]{1,0:T(8,128)(2,1)}, u32[]{:S(2)}) %copy-start) | copy-done | bytes 1048600
  18.7 2.3 %attend_own.1 = (f32[8,512,128]{2,1,0:T(8,128)S(1)}, f32[8,512,256]{2,1,0:T(8,128)S(1)}) custom-call(bf16[512,1024]{1,0:T(8,128)(2,1)S(1)} %copy-done, bf16[1024,128]{1,0:T(8,128)(2,1)S(1)} %constant_dynamic-update-slice_fusion.own_ref, s32[512,128]{1,0:T(8,128)S(1)} %broadcast_in_dim.4.qdoc_ref, s32[1,2048]{1,0:T(1,128)S(1)} %bitcast.7), custom_call_target="tpu_custom_call" | custom-call | flops 4294967296 | bytes 1048576 | tf_op jit(solution)/shard_map/attend_own/pallas_call | solution.py:109
  21.2 7.4 %attend_rest_0.1.refs_0_ = bf16[512,640]{1,0:T(8,128)(2,1)S(1)} custom-call(s32[16]{0:T(128)S(1)} %reshape.4.edge_ref, bf16[512,1024]{1,0:T(8,128)(2,1)S(1)} %copy-done.1, f32[8,512,128]{2,1,0:T(8,128)S(1)} %get-tuple-element.7.peak_ref, f32[8,512,256]{2,1,0:T(8,128)S(1)} %get-tuple-element.8.mix_ref, bf16[1024,128]{1,0:T(8,128)(2,1)S(1)} %get-tuple-element.10.k1_ref, ...), custom_call_target="tpu_custom_call" | custom-call | flops 4294967296 | bytes 1048576 | tf_op jit(solution)/shard_map/attend_rest_0/pallas_call | solution.py:126
  28.6 2.0 %collective-permute-start.4 = (bf16[512,640]{1,0:T(8,128)(2,1)S(1)}, bf16[512,640]{1,0:T(8,128)(2,1)S(1)}, u32[]{:S(2)}, u32[]{:S(2)}) collective-permute-start(bf16[512,640]{1,0:T(8,128)(2,1)S(1)} %attend_rest_0.1.refs_0_), channel_id=1, source_target_pairs={{0,1},{1,2},{2,3},{3,0},{4,5},{5,6},{6,7},{7,4},{8,9},{9,10},{10,1... | collective-permute-start | bytes 1966088 | tf_op jit(solution)/shard_map/ppermute | solution.py:203
  30.6 2.2 %collective-permute-start.7 = (bf16[512,640]{1,0:T(8,128)(2,1)S(1)}, bf16[512,640]{1,0:T(8,128)(2,1)S(1)}, u32[]{:S(2)}, u32[]{:S(2)}) collective-permute-start(bf16[512,640]{1,0:T(8,128)(2,1)S(1)} %attend_rest_0.1.refs_0_), channel_id=1, source_target_pairs={{0,3},{1,0},{2,1},{3,2},{4,7},{5,4},{6,5},{7,6},{8,11},{9,8},{10,9... | collective-permute-start | bytes 1966088 | tf_op jit(solution)/shard_map/ppermute | solution.py:203
  32.8 5.6 %attend_rest_5.1.refs_1_ = bf16[512,384]{1,0:T(8,128)(2,1)S(1)} custom-call(s32[16]{0:T(128)S(1)} %reshape.4.edge_ref, bf16[512,1024]{1,0:T(8,128)(2,1)S(1)} %copy-done.1, f32[8,512,128]{2,1,0:T(8,128)S(1)} %get-tuple-element.7.peak_ref, f32[8,512,256]{2,1,0:T(8,128)S(1)} %get-tuple-element.8.mix_ref, bf16[1024,128]{1,0:T(8,128)(2,1)S(1)} %get-tuple-element.10.k1_ref, ...), custom_call_target="tpu_custom_call" | custom-call | flops 4294967296 | bytes 1048576 | tf_op jit(solution)/shard_map/attend_rest_5/pallas_call | solution.py:126
  38.5 3.2 %collective-permute-start.6 = (bf16[512,384]{1,0:T(8,128)(2,1)S(1)}, bf16[512,384]{1,0:T(8,128)(2,1)S(1)}, u32[]{:S(2)}, u32[]{:S(2)}) collective-permute-start(bf16[512,384]{1,0:T(8,128)(2,1)S(1)} %attend_rest_5.1.refs_1_), channel_id=1, source_target_pairs={{0,3},{1,0},{2,1},{3,2},{4,7},{5,4},{6,5},{7,6},{8,11},{9,8},{10,9... | collective-permute-start | bytes 1179656 | tf_op jit(solution)/shard_map/ppermute | solution.py:203
  41.7 6.6 %collective-permute-done.4.refs_2_ = bf16[512,640]{1,0:T(8,128)(2,1)S(1)} collective-permute-done((bf16[512,640]{1,0:T(8,128)(2,1)S(1)}, bf16[512,640]{1,0:T(8,128)(2,1)S(1)}, u32[]{:S(2)}, u32[]{:S(2)}) %collective-permute-start.4) | collective-permute-done | bytes 655392 | tf_op jit(solution)/shard_map/ppermute | solution.py:203
  48.3 8.4 %collective-permute-done.8.refs_2_.refs_3_ = bf16[512,384]{1,0:T(8,128)(2,1)S(1)} collective-permute-done((bf16[512,384]{1,0:T(8,128)(2,1)S(1)}, bf16[512,384]{1,0:T(8,128)(2,1)S(1)}, u32[]{:S(2)}, u32[]{:S(2)}) %collective-permute-start.8) | collective-permute-done | bytes 393248 | tf_op jit(solution)/shard_map/ppermute | solution.py:203
  56.8 2.1 %collective-permute-start.9 = (bf16[512,384]{1,0:T(8,128)(2,1)S(1)}, bf16[512,384]{1,0:T(8,128)(2,1)S(1)}, u32[]{:S(2)}, u32[]{:S(2)}) collective-permute-start(bf16[512,384]{1,0:T(8,128)(2,1)S(1)} %once_here.1.refs_5_), channel_id=1, source_target_pairs={{0,3},{1,0},{2,1},{3,2},{4,7},{5,4},{6,5},{7,6},{8,11},{9,8},{10,9... | collective-permute-start | bytes 1179656 | tf_op jit(solution)/shard_map/ppermute | solution.py:203
  58.9 11.2 %project_near.1.refs_2_ = f32[512,2048]{1,0:T(8,128)} custom-call(s32[3]{0:T(128)S(1)} %pad_add_fusion.1.at_ref, bf16[512,640]{1,0:T(8,128)(2,1)S(1)} %attend_rest_0.1.refs_0_, bf16[512,384]{1,0:T(8,128)(2,1)S(1)} %attend_rest_5.1.refs_1_, bf16[512,640]{1,0:T(8,128)(2,1)S(1)} %collective-permute-done.4.refs_2_, ...), custom_call_target="tpu_custom_call" | custom-call | flops 1048576 | bytes 1024 | tf_op jit(solution)/shard_map/project_near/pallas_call | solution.py:162
  70.1 0.7 copy-done.2
  70.9 6.7 %project_far.1 = bf16[512,2048]{1,0:T(8,128)(2,1)} custom-call(s32[1]{0:T(128)} %bitcast.at_ref, bf16[512,640]{1,0:T(8,128)(2,1)} %collective-permute-done.5.refs_0_, bf16[512,384]{1,0:T(8,128)(2,1)} %copy-done.2, f32[512,2048]{1,0:T(8,128)} %project_near.1.refs_2_, bf16[4096,2048]{1,0:T(8,128)(2,1)} %refs_3_.1), custom_call_target="tpu_custom_call" | custom-call | flops 1048576 | bytes 1024 | tf_op jit(solution)/shard_map/project_far/pallas_call | solution.py:162
  (20 shorter events, 0.5 us)
Async XLA Ops:
  1.8 19.2 %collective-permute-start.3 = (bf16[1024,128]{1,0:T(8,128)(2,1)S(1)}, bf16[1024,128]{1,0:T(8,128)(2,1)S(1)}, u32[]{:S(2)}, u32[]{:S(2)}) collective-permute-start(bf16[1024,128]{1,0:T(8,128)(2,1)S(1)} %constant_dynamic-update-slice_fusion.own_ref), channel_id=1, source_target_pairs={{4,16},{12,24},{20,32},{28,40},{36,48},{44,56},{52,64},{60,72},{68... | collective-permute-start | bytes 786440 | tf_op jit(solution)/shard_map/ppermute | solution.py:200
  3.1 12.8 %collective-permute-start.1 = (bf16[1024,128]{1,0:T(8,128)(2,1)S(1)}, bf16[1024,128]{1,0:T(8,128)(2,1)S(1)}, u32[]{:S(2)}, u32[]{:S(2)}) collective-permute-start(bf16[1024,128]{1,0:T(8,128)(2,1)S(1)} %constant_dynamic-update-slice_fusion.own_ref), channel_id=1, source_target_pairs={{0,8},{4,12},{8,16},{12,20},{16,24},{20,28},{24,32},{28,36},{32,40... | collective-permute-start | bytes 786440 | tf_op jit(solution)/shard_map/ppermute | solution.py:200
  6.6 14.5 %collective-permute-start = (bf16[1024,128]{1,0:T(8,128)(2,1)S(1)}, bf16[1024,128]{1,0:T(8,128)(2,1)S(1)}, u32[]{:S(2)}, u32[]{:S(2)}) collective-permute-start(bf16[1024,128]{1,0:T(8,128)(2,1)S(1)} %constant_dynamic-update-slice_fusion.own_ref), channel_id=1, source_target_pairs={{0,4},{4,0},{8,12},{12,8},{16,20},{20,16},{24,28},{28,24},{32,36},... | collective-permute-start | bytes 786440 | tf_op jit(solution)/shard_map/ppermute | solution.py:200
  15.9 5.2 %collective-permute-start.2 = (bf16[1024,128]{1,0:T(8,128)(2,1)S(1)}, bf16[1024,128]{1,0:T(8,128)(2,1)S(1)}, u32[]{:S(2)}, u32[]{:S(2)}) collective-permute-start(bf16[1024,128]{1,0:T(8,128)(2,1)S(1)} %collective-permute-done.1.k2_ref), channel_id=1, source_target_pairs={{0,4},{4,0},{8,12},{12,8},{16,20},{20,16},{24,28},{28,24},{32,36},... | collective-permute-start | bytes 786440 | tf_op jit(solution)/shard_map/ppermute | solution.py:200
  17.5 1.2 %copy-start = (bf16[512,1024]{1,0:T(8,128)(2,1)S(1)}, bf16[512,1024]{1,0:T(8,128)(2,1)}, u32[]{:S(2)}) copy-start(bf16[512,1024]{1,0:T(8,128)(2,1)} %q_ref.5) | copy-start | bytes 3145732
  18.7 2.4 %copy-start.1 = (bf16[512,1024]{1,0:T(8,128)(2,1)S(1)}, bf16[512,1024]{1,0:T(8,128)(2,1)}, u32[]{:S(2)}) copy-start(bf16[512,1024]{1,0:T(8,128)(2,1)} %q_ref.5) | copy-start | bytes 3145732
  28.6 19.8 %collective-permute-start.4 = (bf16[512,640]{1,0:T(8,128)(2,1)S(1)}, bf16[512,640]{1,0:T(8,128)(2,1)S(1)}, u32[]{:S(2)}, u32[]{:S(2)}) collective-permute-start(bf16[512,640]{1,0:T(8,128)(2,1)S(1)} %attend_rest_0.1.refs_0_), channel_id=1, source_target_pairs={{0,1},{1,2},{2,3},{3,0},{4,5},{5,6},{6,7},{7,4},{8,9},{9,10},{10,1... | collective-permute-start | bytes 1966088 | tf_op jit(solution)/shard_map/ppermute | solution.py:203
  30.6 26.2 %collective-permute-start.7 = (bf16[512,640]{1,0:T(8,128)(2,1)S(1)}, bf16[512,640]{1,0:T(8,128)(2,1)S(1)}, u32[]{:S(2)}, u32[]{:S(2)}) collective-permute-start(bf16[512,640]{1,0:T(8,128)(2,1)S(1)} %attend_rest_0.1.refs_0_), channel_id=1, source_target_pairs={{0,3},{1,0},{2,1},{3,2},{4,7},{5,4},{6,5},{7,6},{8,11},{9,8},{10,9... | collective-permute-start | bytes 1966088 | tf_op jit(solution)/shard_map/ppermute | solution.py:203
  38.4 18.4 %collective-permute-start.8 = (bf16[512,384]{1,0:T(8,128)(2,1)S(1)}, bf16[512,384]{1,0:T(8,128)(2,1)S(1)}, u32[]{:S(2)}, u32[]{:S(2)}) collective-permute-start(bf16[512,384]{1,0:T(8,128)(2,1)S(1)} %attend_rest_5.1.refs_1_), channel_id=1, source_target_pairs={{0,1},{1,2},{2,3},{3,0},{4,5},{5,6},{6,7},{7,4},{8,9},{9,10},{10,1... | collective-permute-start | bytes 1179656 | tf_op jit(solution)/shard_map/ppermute | solution.py:203
  38.5 18.3 %collective-permute-start.6 = (bf16[512,384]{1,0:T(8,128)(2,1)S(1)}, bf16[512,384]{1,0:T(8,128)(2,1)S(1)}, u32[]{:S(2)}, u32[]{:S(2)}) collective-permute-start(bf16[512,384]{1,0:T(8,128)(2,1)S(1)} %attend_rest_5.1.refs_1_), channel_id=1, source_target_pairs={{0,3},{1,0},{2,1},{3,2},{4,7},{5,4},{6,5},{7,6},{8,11},{9,8},{10,9... | collective-permute-start | bytes 1179656 | tf_op jit(solution)/shard_map/ppermute | solution.py:203
  48.3 21.8 %collective-permute-start.5 = (bf16[512,640]{1,0:T(8,128)(2,1)S(1)}, bf16[512,640]{1,0:T(8,128)(2,1)}, u32[]{:S(2)}, u32[]{:S(2)}) collective-permute-start(bf16[512,640]{1,0:T(8,128)(2,1)S(1)} %collective-permute-done.4.refs_2_), channel_id=1, source_target_pairs={{0,1},{1,2},{2,3},{3,0},{4,5},{5,6},{6,7},{7,4},{8,9},{9,10},{10,1... | collective-permute-start | bytes 1966088 | tf_op jit(solution)/shard_map/ppermute | solution.py:203
  56.8 13.4 %collective-permute-start.9 = (bf16[512,384]{1,0:T(8,128)(2,1)S(1)}, bf16[512,384]{1,0:T(8,128)(2,1)S(1)}, u32[]{:S(2)}, u32[]{:S(2)}) collective-permute-start(bf16[512,384]{1,0:T(8,128)(2,1)S(1)} %once_here.1.refs_5_), channel_id=1, source_target_pairs={{0,3},{1,0},{2,1},{3,2},{4,7},{5,4},{6,5},{7,6},{8,11},{9,8},{10,9... | collective-permute-start | bytes 1179656 | tf_op jit(solution)/shard_map/ppermute | solution.py:203
  70.1 0.8 copy-start.2
